TPU v7x, 32 devices: a whole 2x2x4 slice. The times are simulated.
32 devices in a mesh: dp: 8 (over y, x, core), expert: 4 (over z).
Axes of the slice: x: 2, y: 2, z: 4, core: 2. Of those that a mesh axis runs over, the one named last changes fastest.
Arguments:
- expert_partials: float32 [8, 4, 1536, 2048], P('dp', 'expert'), may hold values from -5 to 5
- key_partials: float32 [8, 512, 4096], P('dp', None, 'expert'), may hold values from -5 to 5
- expert_param: float32 [4, 1536, 2048], P('expert', 'dp'), may hold values from -0.3125 to 0.3125
- expert_moment: float32 [4, 1536, 2048], P('expert', 'dp'), may hold values from -4 to 4
- expert_second: float32 [4, 1536, 2048], P('expert', 'dp'), may hold values from 0.05 to 1
- key_param: float32 [512, 4096], P('dp', 'expert'), may hold values from -0.3125 to 0.3125
- key_moment: float32 [512, 4096], P('dp', 'expert'), may hold values from -4 to 4
- key_second: float32 [512, 4096], P('dp', 'expert'), may hold values from 0.05 to 1
- expert_scales: float32 [4, 12, 16], replicated, may hold values from 0.0001 to 0.001
- key_scales: float32 [4, 32], P(None, 'expert'), may hold values from 0.0001 to 0.001
- rotary_order: int32 [128], replicated, may hold values from 0 to 127, each once
- expert_slot: int32 [4], replicated, may hold values from 0 to 3, each once
Outputs:
- new_expert_param: float32 [4, 1536, 2048], P('expert', 'dp')
- new_expert_moment: float32 [4, 1536, 2048], P('expert', 'dp')
- new_expert_second: float32 [4, 1536, 2048], P('expert', 'dp')
- new_key_param: float32 [512, 4096], P('dp', 'expert')
- new_key_moment: float32 [512, 4096], P('dp', 'expert')
- new_key_second: float32 [512, 4096], P('dp', 'expert')
- server_expert: bfloat16 [4, 2048, 1536], P(None, 'expert', 'dp')
- server_key: bfloat16 [4096, 512], P('expert')
Inputs may be any that keep to these rules, and one draw needn't show every extreme that they name: `rotary_order`: a permutation of the rows of one head. `expert_slot`: a permutation of the experts.
All inputs are finite; a program needn't handle non-finite values.
Results may differ from a plain program's by a relative error of at most 0.007.
Values may be sent and summed in bfloat16 or wider, within the bound.
A program may use at most 128 MiB of HBM per device.

v0:
```python
import jax
import jax.numpy as jnp
from jax import lax
from jax.sharding import PartitionSpec as P

HD = 128
BLOCK = 128


BETA_ONE = 0.9
BETA_TWO = 0.95
LEARN = 0.01
DECAY = 0.1
EPSILON = 1e-08
LIMIT = 448.0
CORRECT_ONE = 1.0 - 0.9**10
CORRECT_TWO = 1.0 - 0.95**10


def adam_update(param, moment, second, grad):
    moment = BETA_ONE * moment + (1.0 - BETA_ONE) * grad
    second = BETA_TWO * second + (1.0 - BETA_TWO) * grad * grad
    corrected = moment / CORRECT_ONE / (jnp.sqrt(second / CORRECT_TWO) + EPSILON)
    return (param * (1.0 - LEARN * DECAY) - LEARN * corrected, moment, second)


def to_grid(weights, scales):
    return jnp.clip(weights / scales, -LIMIT, LIMIT).astype(jnp.bfloat16)


def on_device(
    expert_partials,
    key_partials,
    expert_param,
    expert_moment,
    expert_second,
    key_param,
    key_moment,
    key_second,
    expert_scales,
    key_scales,
    rotary_order,
    expert_slot,
):
    dp_index = lax.axis_index("dp")
    expert_index = lax.axis_index("expert")
    expert_grad, key_grad = (
        lax.psum_scatter(
            expert_partials.astype(jnp.bfloat16), "dp", scatter_dimension=2, tiled=True
        ).astype(jnp.float32),
        lax.psum_scatter(
            key_partials.astype(jnp.bfloat16), "dp", scatter_dimension=1, tiled=True
        ).astype(jnp.float32),
    )
    new_ep, new_em, new_es = adam_update(expert_param, expert_moment, expert_second, expert_grad[0])
    local_experts, row_count, width = new_ep.shape
    row_blocks = (dp_index * row_count + jnp.arange(row_count, dtype=jnp.int32)) // BLOCK
    row_scales = jnp.take(expert_scales, row_blocks, axis=1)
    arrived = lax.all_to_all(new_ep, "expert", split_axis=2, concat_axis=0, tiled=True)
    columns = arrived.shape[2]
    column_scales = lax.dynamic_slice_in_dim(
        row_scales, expert_index * (columns // BLOCK), columns // BLOCK, 2
    )
    grid_blocks = to_grid(arrived, jnp.repeat(column_scales, BLOCK, axis=2))
    transposed = jnp.transpose(grid_blocks, (0, 2, 1))
    server_expert = jnp.zeros_like(transposed).at[expert_slot].set(transposed)
    new_kp, new_km, new_ks = adam_update(key_param, key_moment, key_second, key_grad[0])
    column_full = jnp.repeat(key_scales, BLOCK, axis=1)
    gathered = lax.all_gather(new_kp, "dp", axis=0, tiled=True)
    key_grid = to_grid(gathered, jnp.repeat(column_full, BLOCK, axis=0))
    total_rows = key_grid.shape[0]
    all_rows = jnp.arange(total_rows, dtype=jnp.int32)
    source = all_rows // HD * HD + rotary_order[all_rows % HD]
    server_key = jnp.take(key_grid, source, axis=0).T
    return (new_ep, new_em, new_es, new_kp, new_km, new_ks, server_expert, server_key)


def solution(mesh):
    return jax.shard_map(
        on_device,
        mesh=mesh,
        in_specs=(
            P("dp", "expert", None, None),
            P("dp", None, "expert"),
            P("expert", "dp", None),
            P("expert", "dp", None),
            P("expert", "dp", None),
            P("dp", "expert"),
            P("dp", "expert"),
            P("dp", "expert"),
            P(),
            P(None, "expert"),
            P(),
            P(),
        ),
        out_specs=(
            P("expert", "dp", None),
            P("expert", "dp", None),
            P("expert", "dp", None),
            P("dp", "expert"),
            P("dp", "expert"),
            P("dp", "expert"),
            P(None, "expert", "dp"),
            P("expert", None),
        ),
        check_vma=False,
    )
```

profile of v0, /device:TPU:0, one launch (start us, length us, event | category | flops | bytes accessed | tf_op | source)
XLA Modules:
  0.0 314.3 jit_solution(9243599890408515266)
XLA Ops:
  7.2 0.0 copy-start
  7.2 0.0 reduce-scatter.2.cloned.1.call-start
  7.2 2.7 convert_element_type.15
  10.0 0.0 reduce-scatter.2.cloned.1.call-update
  10.0 0.0 all-reduce.3.cloned.1.call-start
  10.0 15.4 %copy.62 = bf16[1,1,1536,2048]{3,1,0,2:T(2,128)(2,1)} copy(f32[1,1,1536,2048]{3,2,1,0:T(8,128)} %param.12) | data formatting | bytes 18874368 | tf_op args[0]
  25.4 0.0 copy-start.7
  25.5 0.0 copy-start.8
  25.5 0.0 all-reduce.3.cloned.1.call-update
  25.5 0.0 copy-start.5
  25.5 0.0 all-gather.2.cloned.1.call-start
  25.6 0.5 copy-done.11
  26.1 0.6 dynamic-slice.1
  27.3 23.2 %reduce-scatter.2.cloned.1.call-done = bf16[1,64,1024]{2,1,0:T(8,128)(2,1)} async-done(((bf16[1,512,1024]{2,1,0:T(8,128)(2,1)}), bf16[1,64,1024]{2,1,0:T(8,128)(2,1)}) %reduce-scatter.2.cloned.1.call-update) | async-done | bytes 131088 | tf_op jit(solution)/shard_map/reduce_scatter | solution.py:51
  50.5 0.0 copy-done.6
  50.5 0.0 copy-done.7
  50.5 0.0 copy-done.8
  50.5 1.9 multiply_subtract_fusion
  52.4 0.0 all-gather.2.cloned.1.call-update
  52.5 173.8 %all-reduce.3.cloned.1.call-done = bf16[1,1,1536,2048]{3,1,0,2:T(2,128)(2,1)} async-done(((bf16[1,1,1536,2048]{3,1,0,2:T(2,128)(2,1)}), bf16[1,1,1536,2048]{3,1,0,2:T(2,128)(2,1)}) %all-reduce.3.cloned.1.call-update) | async-done | bytes 6291472
  226.3 0.0 copy-done.5
  226.3 14.4 %fusion.6 = (f32[1,192,2048]{2,0,1:T(1,128)S(1)}, f32[1,192,2048]{2,0,1:T(1,128)}, f32[1,192,2048]{2,0,1:T(1,128)}) fusion(f32[1,192,2048]{2,1,0:T(8,128)S(1)} %copy-done.5, bf16[1,1,1536,2048]{3,1,0,2:T(2,128)(2,1)} %all-reduce.3.cloned.1.call-done, u32[]{:T(128)S(6)} %multiply.5, f32[1,192,2048]{2,1,0:T(8,128)} %param.15, f32[1,192,2048]{2,1,0:T(8,128)} %param.16), kind=kLoop, calls=%fused_computation.18 | loop fusion | flops 5898240 | bytes 10223620 | tf_op jit(solution)/shard_map/sub | solution.py:24
  240.7 5.7 %copy.43 = f32[1,192,2048]{1,0,2:T(1,128)} copy(f32[1,192,2048]{2,0,1:T(1,128)S(1)} %get-tuple-element.43) | data formatting | bytes 3145728 | tf_op jit(solution)/shard_map/sub | solution.py:24
  246.4 4.6 %all-to-all-start = ((f32[1,192,2048]{1,0,2:T(1,128)}), f32[1,192,2048]{1,0,2:T(1,128)}, u32[]{:S(2)}, u32[]{:S(2)}) async-start(f32[1,192,2048]{1,0,2:T(1,128)} %copy.43), calls=%async_computation.1 | async-start | bytes 4194304 | tf_op jit(solution)/shard_map/all_to_all | solution.py:59
  251.0 0.9 gather_fusion
  251.9 0.5 fusion.8
  252.4 1.8 broadcast_in_dim.40
  254.3 2.0 reshape.212
  256.3 0.0 copy-done.9
  256.3 0.0 copy-start.10
  256.3 0.1 broadcast_bitcast_fusion
  256.4 3.3 %gather_fusion.1 = s32[512]{0:T(512)S(1)} fusion(s32[128]{0:T(128)S(1)} %copy-done.1, s32[1024]{0:T(1024)S(1)} %pad_clamp_fusion.1), kind=kCustom, calls=%fused_computation.1 | custom fusion | bytes 6144 | tf_op jit(solution)/shard_map/gather | solution.py:73
  259.8 0.0 copy-start.3
  259.8 1.7 copy.46
  261.6 1.7 copy.47
  263.3 0.0 copy-done.2
  263.3 1.7 copy.48
  265.1 1.9 fusion.1
  266.9 2.8 gather_fusion.2
  269.7 1.4 select_bitcast_fusion
  271.1 1.3 copy.49
  272.4 26.8 %all-to-all-done = f32[1,192,2048]{1,0,2:T(1,128)} async-done(((f32[1,192,2048]{1,0,2:T(1,128)}), f32[1,192,2048]{1,0,2:T(1,128)}, u32[]{:S(2)}, u32[]{:S(2)}) %all-to-all-start) | async-done | bytes 1572896 | tf_op jit(solution)/shard_map/all_to_all | solution.py:59
  299.3 4.5 %copy.44 = f32[1,192,4,512]{3,1,2,0:T(8,128)S(1)} copy(f32[1,192,4,512]{1,0,3,2:T(1,128)} %bitcast.5) | data formatting | bytes 3145728 | tf_op jit(solution)/shard_map/all_to_all | solution.py:59
  303.7 1.3 fusion.7
  305.0 0.1 broadcast_in_dim.36
  305.1 1.8 scatter_fusion
  306.9 0.0 copy-start.4
  306.9 0.9 copy-done.4
  (21 shorter events, 0.1 us)
Async XLA Ops:
  7.2 243.9 %copy-start = (f32[4,12,16]{2,0,1:T(4,128)S(1)}, f32[4,12,16]{2,0,1:T(4,128)}, u32[]{:S(2)}) copy-start(f32[4,12,16]{2,0,1:T(4,128)} %param.20) | copy-start | bytes 9220
  7.2 43.3 %reduce-scatter.2.cloned.1.call-start = ((), (), s32[]{:S(2)}) async-start(), calls=%async_computation.2 | async-start | bytes 1179648 | tf_op jit(solution)/shard_map/reduce_scatter | solution.py:51
  10.0 216.3 %all-reduce.3.cloned.1.call-start = ((), (), s32[]{:S(2)}) async-start(), calls=%async_computation.4 | async-start | bytes 25165824
  25.4 0.7 copy-start.11
  25.4 25.1 %copy-start.6 = (f32[64,1024]{1,0:T(8,128)S(1)}, f32[64,1024]{1,0:T(8,128)}, u32[]{:S(2)}) copy-start(f32[64,1024]{1,0:T(8,128)} %param.17) | copy-start | bytes 786436
  25.4 25.1 %copy-start.7 = (f32[64,1024]{1,0:T(8,128)S(1)}, f32[64,1024]{1,0:T(8,128)}, u32[]{:S(2)}) copy-start(f32[64,1024]{1,0:T(8,128)} %param.18) | copy-start | bytes 786436
  25.5 25.1 %copy-start.8 = (f32[64,1024]{1,0:T(8,128)S(1)}, f32[64,1024]{1,0:T(8,128)}, u32[]{:S(2)}) copy-start(f32[64,1024]{1,0:T(8,128)} %param.19) | copy-start | bytes 786436
  25.5 200.8 %copy-start.5 = (f32[1,192,2048]{2,1,0:T(8,128)S(1)}, f32[1,192,2048]{2,1,0:T(8,128)}, u32[]{:S(2)}) copy-start(f32[1,192,2048]{2,1,0:T(8,128)} %param.14) | copy-start | bytes 4718596
  25.5 239.6 %all-gather.2.cloned.1.call-start = ((), (), s32[]{:S(2)}) async-start(), calls=%async_computation.3 | async-start | bytes 2359296 | tf_op jit(solution)/shard_map/all_gather | solution.py:69
  246.4 52.9 %all-to-all-start = ((f32[1,192,2048]{1,0,2:T(1,128)}), f32[1,192,2048]{1,0,2:T(1,128)}, u32[]{:S(2)}, u32[]{:S(2)}) async-start(f32[1,192,2048]{1,0,2:T(1,128)} %copy.43), calls=%async_computation.1 | async-start | bytes 4194304 | tf_op jit(solution)/shard_map/all_to_all | solution.py:59
  254.3 2.0 copy-start.9
  254.3 2.1 copy-start.1
  256.3 3.5 %copy-start.10 = (s32[4]{0:T(128)S(1)}, s32[4]{0:T(128)}, u32[]{:S(2)}) copy-start(s32[4]{0:T(128)} %param.23) | copy-start | bytes 52
  259.8 1.8 copy-start.3
  261.6 1.8 copy-start.2
  306.9 0.9 copy-start.4
Sparse Core Ops, SparseCore 0:
  11.8 38.7 reduce-scatter.1
  54.0 172.2 all-reduce.2
  228.9 27.9 all-gather.1
where the time goes:
time: 315 us; the launch traced here: 314 us
  waiting for transfers between devices  224 us (71%)
  local copies, waits for them, and re-layouts  46.9 us (15%)
  other arithmetic  24.1 us (8%)
  between operations  14.6 us (5%)
  starting transfers between devices  4.72 us (1%)
    unnamed x4, waiting for transfers between devices  174 us
    all_to_all x1, waiting for transfers between devices, on_device(): lax.all_to_all(new_ep, 'expert', split_axis=2, concat_axis=0, tiled=True)  26.8 us
    unnamed x32, local copies, waits for them, and re-layouts  24.1 us
    reduce_scatter x1, waiting for transfers between devices, on_device(): lax.psum_scatter(key_partials.astype(jnp.bfloat16), 'dp', scatter_dimensi...  23.2 us
    sub x2, other arithmetic, adam_update(): return (param * (1.0 - LEARN * DECAY) - LEARN * corrected, moment, second)  16.3 us
  transfers between devices with their start and end apart: 4, of which 3 were waited for; matrix products, arithmetic and copies ran while one was open for 19% of the time, Pallas kernels for 0%

commit v1 on v0

v1 whole, which is shorter than its diff:
```python
import functools
import math

import jax
import jax.numpy as jnp
from jax import lax
from jax.experimental import pallas as pl
from jax.experimental.pallas import tpu as pltpu
from jax.sharding import PartitionSpec as P

HD = 128
BLOCK = 128
BETA_ONE = 0.9
BETA_TWO = 0.95
LEARN = 0.01
DECAY = 0.1
EPSILON = 1e-08
LIMIT = 448.0
CORRECT_ONE = 1.0 - 0.9**10
CORRECT_TWO = 1.0 - 0.95**10
MESH = pl.DeviceIdType.MESH
F32 = jnp.float32
BF16 = jnp.bfloat16


def adam_update(param, moment, second, grad):
    moment = BETA_ONE * moment + (1.0 - BETA_ONE) * grad
    second = BETA_TWO * second + (1.0 - BETA_TWO) * grad * grad
    scaled = moment * (1.0 / CORRECT_ONE)
    corrected = scaled / (jnp.sqrt(second * (1.0 / CORRECT_TWO)) + EPSILON)
    return (param * (1.0 - LEARN * DECAY) - LEARN * corrected, moment, second)


def loop(count, body):
    def step(i, carry):
        body(i)
        return carry

    lax.fori_loop(0, count, step, 0)


def kernel(
    n_dp,
    n_ex,
    eg_hbm,
    kg_hbm,
    ep_hbm,
    em_hbm,
    es_hbm,
    kp_hbm,
    km_hbm,
    ks_hbm,
    e_scale,
    k_scale,
    order,
    o_ep,
    o_em,
    o_es,
    o_kp,
    o_km,
    o_ks,
    o_arr,
    o_key,
    e_far,
    e_own,
    e_s0s,
    e_s0r,
    e_state,
    e_grid,
    k_far,
    k_own,
    k_s0s,
    k_s0r,
    k_state,
    k_gath,
    k_out,
    *rest,
):
    chips = n_dp // 2
    m = chips.bit_length() - 1
    rest = list(rest)
    e_snd = [rest.pop(0) for _ in range(m)]
    e_rcv = [rest.pop(0) for _ in range(m)]
    k_snd = [rest.pop(0) for _ in range(m)]
    k_rcv = [rest.pop(0) for _ in range(m)]
    load_sem, s0_sem, rs_sem, out_sem, a2a_sem, ag_sem, pair_sem, key_sem = rest

    d = lax.axis_index("dp")
    z = lax.axis_index("expert")
    core = d % 2
    chip = d // 2
    bits = [(chip // 2**i) % 2 for i in range(m)]

    def chip_of(values):
        total = values[0] * 1
        for i in range(1, m):
            total = total + values[i] * 2**i
        return total

    def partner(i):
        return d + (1 - 2 * bits[i]) * 2 ** (i + 1)

    other_core = d + 1 - 2 * core
    orders = (list(range(m)), list(range(m))[::-1])

    rows, width = ep_hbm.shape[1:]
    krows, kwidth = kp_hbm.shape
    cw = width // n_ex

    def place(t):
        return (z + n_ex - 1 - t) % n_ex

    class Unit:
        pass

    units = []
    for u in range(n_ex + 1):
        w = Unit()
        w.u = u
        if u == 0:
            w.rows, w.cols = krows, kwidth
            w.columns = pl.ds(0, kwidth)
            w.far, w.own, w.s0s, w.s0r = k_far, k_own, k_s0s, k_s0r
            w.snd, w.rcv = k_snd, k_rcv
            w.grad = kg_hbm
            w.state = [k_state.at[i] for i in range(3)]
            w.state_in = [kp_hbm, km_hbm, ks_hbm]
            w.state_out = [o_kp, o_km, o_ks]
        else:
            t = u - 1
            w.dest = place(t)
            w.rows, w.cols = rows, cw
            w.columns = pl.ds(pl.multiple_of(w.dest * cw, cw), cw)
            w.far, w.own, w.s0s, w.s0r = (r.at[t] for r in (e_far, e_own, e_s0s, e_s0r))
            w.snd = [r.at[t] for r in e_snd]
            w.rcv = [r.at[t] for r in e_rcv]
            w.grad = eg_hbm
            w.state = [e_state.at[t, i] for i in range(3)]
            w.state_in = [r.at[0, :, w.columns] for r in (ep_hbm, em_hbm, es_hbm)]
            w.state_out = [r.at[0, :, w.columns] for r in (o_ep, o_em, o_es)]
        w.half = w.cols // 2
        w.load_far = pltpu.make_async_copy(
            w.grad.at[:, 1 - core, :, w.columns], w.far, load_sem.at[u, 0]
        )
        w.load_own = pltpu.make_async_copy(
            w.grad.at[:, core, :, w.columns], w.own, load_sem.at[u, 1]
        )
        w.load_state = [
            pltpu.make_async_copy(w.state_in[i], w.state[i], load_sem.at[u, 2 + i])
            for i in range(3)
        ]
        w.store_state = [
            pltpu.make_async_copy(w.state[i], w.state_out[i], out_sem.at[u, i])
            for i in range(3)
        ]
        w.s0 = pltpu.make_async_remote_copy(
            src_ref=w.s0s,
            dst_ref=w.s0r,
            send_sem=s0_sem.at[u, 0],
            recv_sem=s0_sem.at[u, 1],
            device_id=(other_core, z),
            device_id_type=MESH,
        )
        w.rs = [
            [
                pltpu.make_async_remote_copy(
                    src_ref=w.snd[s].at[h],
                    dst_ref=w.rcv[s].at[h],
                    send_sem=rs_sem.at[u, s, h, 0],
                    recv_sem=rs_sem.at[u, s, h, 1],
                    device_id=(partner(orders[h][s]), z),
                    device_id_type=MESH,
                )
                for h in range(2)
            ]
            for s in range(m)
        ]
        units.append(w)

    for w in units:
        w.load_far.start()
        w.load_own.start()
    for w in units:
        for c in w.load_state:
            c.start()

    barrier = pltpu.get_barrier_semaphore()
    peers = [(other_core, z)] + [(partner(i), z) for i in range(m)]
    peers += [(d, (z + k) % n_ex) for k in range(1, n_ex)]
    for peer in peers:
        pl.semaphore_signal(barrier, inc=1, device_id=peer, device_id_type=MESH)
    pl.semaphore_wait(barrier, len(peers))

    def index_in(values, h, s):
        total = 0
        for k, b in enumerate(orders[h][s + 1 :]):
            total = total + values[b] * 2**k
        return total

    def block_sum(w, values, h, s, r):
        q = chip_of(values)
        lanes = slice(h * w.half, (h + 1) * w.half)
        total = w.own[q, r, lanes] + w.s0r[q, r, lanes].astype(F32)
        for past in range(s):
            total = total + w.rcv[past][h, index_in(values, h, past), r, :].astype(F32)
        return total

    def first(w):
        w.load_far.wait()
        step = math.gcd(w.rows, 16384 // w.cols)
        per = w.rows // step

        def body(i):
            q = i // per
            r = pl.ds(pl.multiple_of((i % per) * step, step), step)
            w.s0s[q, r, :] = w.far[q, r, :].astype(BF16)

        loop(chips * per, body)
        w.s0.start()

    def reduce(w, s):
        if s == 0:
            w.load_own.wait()
            w.s0.wait_recv()
        step = math.gcd(w.rows, 16384 // w.half)
        for h in range(2):
            if s > 0:
                w.rs[s - 1][h].wait_recv()
            left = orders[h][s + 1 :]
            for slot in range(2 ** len(left)):
                values = list(bits)
                values[orders[h][s]] = 1 - bits[orders[h][s]]
                for k, b in enumerate(left):
                    values[b] = (slot >> k) & 1

                def body(i):
                    r = pl.ds(pl.multiple_of(i * step, step), step)
                    w.snd[s][h, slot, r, :] = block_sum(w, values, h, s, r).astype(BF16)

                loop(w.rows // step, body)
            w.rs[s][h].start()

    def update(w):
        for c in w.load_state:
            c.wait()
        step = math.gcd(w.rows, 8192 // w.half)
        for h in range(2):
            w.rs[m - 1][h].wait_recv()

            def body(i):
                r = pl.ds(pl.multiple_of(i * step, step), step)
                lanes = slice(h * w.half, (h + 1) * w.half)
                grad = block_sum(w, bits, h, m, r)
                new = adam_update(*(ref[r, lanes] for ref in w.state), grad)
                for ref, value in zip(w.state, new):
                    ref[r, lanes] = value
                block = (d * w.rows + i * step) // BLOCK
                for j in range(w.half // BLOCK):
                    at = h * (w.half // BLOCK) + j
                    if w.u == 0:
                        scale = k_scale[block, at]
                    else:
                        scale = e_scale[z, block, w.dest * (cw // BLOCK) + at]
                    part = new[0][:, j * BLOCK : (j + 1) * BLOCK] / scale
                    part = jnp.clip(part, -LIMIT, LIMIT)
                    cols = slice(at * BLOCK, (at + 1) * BLOCK)
                    if w.u == 0:
                        k_gath[chip, core, r, cols] = part.astype(BF16)
                    else:
                        e_grid[w.u - 1, r, cols] = part.astype(BF16)

            loop(w.rows // step, body)
        for c in w.store_state:
            c.start()
        if w.u == 0:
            gather_send(0)
        else:
            a2a(w.u - 1).start()

    def a2a(t):
        if t == n_ex - 1:
            return pltpu.make_async_copy(e_grid.at[t], o_arr.at[z], a2a_sem.at[t, 0])
        return pltpu.make_async_remote_copy(
            src_ref=e_grid.at[t],
            dst_ref=o_arr.at[z],
            send_sem=a2a_sem.at[t, 0],
            recv_sem=a2a_sem.at[t, 1],
            device_id=(d, place(t)),
            device_id_type=MESH,
        )

    khalf = kwidth // 2

    def gather_copies(s):
        copies = []
        for h in range(2):
            done = orders[h][:s]
            for slot in range(2**s):
                values = list(bits)
                for k, b in enumerate(done):
                    values[b] = (slot >> k) & 1
                ref = k_gath.at[chip_of(values), core, :, pl.ds(h * khalf, khalf)]
                copies.append(
                    pltpu.make_async_remote_copy(
                        src_ref=ref,
                        dst_ref=ref,
                        send_sem=ag_sem.at[s, h, slot, 0],
                        recv_sem=ag_sem.at[s, h, slot, 1],
                        device_id=(partner(orders[h][s]), z),
                        device_id_type=MESH,
                    )
                )
        return copies

    pair = pltpu.make_async_remote_copy(
        src_ref=k_gath.at[:, core],
        dst_ref=k_gath.at[:, core],
        send_sem=pair_sem.at[0],
        recv_sem=pair_sem.at[1],
        device_id=(other_core, z),
        device_id_type=MESH,
    )
    store_key = pltpu.make_async_copy(k_out, o_key, key_sem.at[0])

    def gather_send(s):
        for c in gather_copies(s):
            c.start()

    def gather_next(s):
        for c in gather_copies(s):
            c.wait_recv()
        if s + 1 < m:
            gather_send(s + 1)
        else:
            pair.start()

    def key_finish():
        pair.wait_recv()
        source = lax.broadcasted_iota(jnp.int32, (HD, HD), 0)
        pick = jnp.where(source == order[...], 1.0, 0.0).astype(BF16)
        span = HD // (2 * krows)
        wide = 256
        for head in range(k_out.shape[1] // HD):
            for j in range(kwidth // wide):
                cols = slice(j * wide, (j + 1) * wide)
                block = k_gath[head * span : (head + 1) * span, :, :, cols].reshape(HD, wide)
                turned = lax.dot_general(
                    block, pick, (((0,), (0,)), ((), ())), preferred_element_type=F32
                )
                k_out[cols, head * HD : (head + 1) * HD] = turned.astype(BF16)
        store_key.start()

    stages = [first] + [functools.partial(reduce, s=s) for s in range(m)] + [update]
    extra = [functools.partial(gather_next, s) for s in range(m)] + [key_finish]
    for slot in range(len(units) + len(stages) - 1):
        for s, stage in enumerate(stages):
            if 0 <= slot - s < len(units):
                stage(units[slot - s])
        if 0 <= slot - len(stages) < len(extra):
            extra[slot - len(stages)]()
    for task in extra[len(units) - 1 :]:
        task()

    for t in range(n_ex):
        if t == n_ex - 1:
            a2a(t).wait()
        else:
            a2a(t).wait_send()
            a2a(t).wait_recv()
    for w in units:
        w.s0.wait_send()
        for s in range(m):
            for h in range(2):
                w.rs[s][h].wait_send()
        for c in w.store_state:
            c.wait()
    for s in range(m):
        for c in gather_copies(s):
            c.wait_send()
    pair.wait_send()
    store_key.wait()


def place_slots(n_ex, slot, arrived, placed, sems):
    copies = [
        pltpu.make_async_copy(arrived.at[e], placed.at[slot[e]], sems.at[e]) for e in range(n_ex)
    ]
    for c in copies:
        c.start()
    for c in copies:
        c.wait()


def solution(mesh):
    n_dp, n_ex = mesh.shape["dp"], mesh.shape["expert"]

    def on_device(
        expert_partials,
        key_partials,
        expert_param,
        expert_moment,
        expert_second,
        key_param,
        key_moment,
        key_second,
        expert_scales,
        key_scales,
        rotary_order,
        expert_slot,
    ):
        chips = n_dp // 2
        m = chips.bit_length() - 1
        _, rows, width = expert_param.shape
        krows, kwidth = key_param.shape
        key_rows = key_partials.shape[1]
        cw = width // n_ex
        eg = expert_partials.reshape(chips, 2, rows, width)
        kg = key_partials.reshape(chips, 2, krows, kwidth)
        shape = jax.ShapeDtypeStruct
        anywhere = pl.BlockSpec(memory_space=pl.ANY)
        scalars = pl.BlockSpec(memory_space=pltpu.SMEM)
        vector = pl.BlockSpec(memory_space=pltpu.VMEM)
        dma = pltpu.SemaphoreType.DMA
        counts = [2 ** (m - 1 - s) for s in range(m)]
        out = pl.pallas_call(
            functools.partial(kernel, n_dp, n_ex),
            out_shape=[shape(expert_param.shape, F32)] * 3
            + [shape(key_param.shape, F32)] * 3
            + [shape((n_ex, rows, cw), BF16), shape((kwidth, key_rows), BF16)],
            in_specs=[anywhere] * 8 + [scalars] * 2 + [vector],
            out_specs=[anywhere] * 8,
            scratch_shapes=[
                pltpu.VMEM((n_ex, chips, rows, cw), F32),
                pltpu.VMEM((n_ex, chips, rows, cw), F32),
                pltpu.VMEM((n_ex, chips, rows, cw), BF16),
                pltpu.VMEM((n_ex, chips, rows, cw), BF16),
                pltpu.VMEM((n_ex, 3, rows, cw), F32),
                pltpu.VMEM((n_ex, rows, cw), BF16),
                pltpu.VMEM((chips, krows, kwidth), F32),
                pltpu.VMEM((chips, krows, kwidth), F32),
                pltpu.VMEM((chips, krows, kwidth), BF16),
                pltpu.VMEM((chips, krows, kwidth), BF16),
                pltpu.VMEM((3, krows, kwidth), F32),
                pltpu.VMEM((chips, 2, krows, kwidth), BF16),
                pltpu.VMEM((kwidth, key_rows), BF16),
            ]
            + [pltpu.VMEM((n_ex, 2, c, rows, cw // 2), BF16) for c in counts] * 2
            + [pltpu.VMEM((2, c, krows, kwidth // 2), BF16) for c in counts] * 2
            + [
                dma((n_ex + 1, 5)),
                dma((n_ex + 1, 2)),
                dma((n_ex + 1, m, 2, 2)),
                dma((n_ex + 1, 3)),
                dma((n_ex, 2)),
                dma((m, 2, 2 ** (m - 1), 2)),
                dma((2,)),
                dma((1,)),
            ],
            compiler_params=pltpu.CompilerParams(
                collective_id=0, has_side_effects=True, vmem_limit_bytes=58 * 2**20
            ),
            name="reduce_update_exchange",
        )(
            eg,
            kg,
            expert_param,
            expert_moment,
            expert_second,
            key_param,
            key_moment,
            key_second,
            expert_scales,
            key_scales,
            rotary_order.reshape(1, HD),
        )
        new_ep, new_em, new_es, new_kp, new_km, new_ks, arrived, server_key = out
        placed = pl.pallas_call(
            functools.partial(place_slots, n_ex),
            out_shape=shape(arrived.shape, BF16),
            in_specs=[scalars, anywhere],
            out_specs=anywhere,
            scratch_shapes=[dma((n_ex,))],
            name="place_slots",
        )(expert_slot, arrived)
        server_expert = jnp.transpose(placed, (0, 2, 1))
        return (new_ep, new_em, new_es, new_kp, new_km, new_ks, server_expert, server_key)

    return jax.shard_map(
        on_device,
        mesh=mesh,
        in_specs=(
            P("dp", "expert", None, None),
            P("dp", None, "expert"),
            P("expert", "dp", None),
            P("expert", "dp", None),
            P("expert", "dp", None),
            P("dp", "expert"),
            P("dp", "expert"),
            P("dp", "expert"),
            P(),
            P(None, "expert"),
            P(),
            P(),
        ),
        out_specs=(
            P("expert", "dp", None),
            P("expert", "dp", None),
            P("expert", "dp", None),
            P("dp", "expert"),
            P("dp", "expert"),
            P("dp", "expert"),
            P(None, "expert", "dp"),
            P("expert", None),
        ),
        check_vma=False,
    )
```

time: 315 us -> 87.3 us (0.28)
  waiting for transfers between devices: 224 us -> 0 us
  Pallas kernels: 0 us -> 76.7 us
  local copies, waits for them, and re-layouts: 46.9 us -> 9.54 us
  other arithmetic: 24.1 us -> 0 us
  between operations: 14.6 us -> 0.68 us
  starting transfers between devices: 4.72 us -> 0 us
    unnamed x4 -> x0, waiting for transfers between devices: 174 us -> none
    pallas_call x0 -> x2, Pallas kernels: none -> 76.7 us  [the longest x1 50.9 us: on_device(): pl.pallas_call(functools.partial(kernel, n_dp, n_ex), out_shape=[shape(ex...]
    all_to_all x1 -> x0, waiting for transfers between devices: 26.8 us -> none  [on_device(): lax.all_to_all(new_ep, 'expert', split_axis=2, concat_axis=0, tiled=True)]
    reduce_scatter x1 -> x0, waiting for transfers between devices: 23.2 us -> none  [on_device(): lax.psum_scatter(key_partials.astype(jnp.bfloat16), 'dp', scatter_dimensi...]
    sub x2 -> x0, other arithmetic: 16.3 us -> none  [adam_update(): return (param * (1.0 - LEARN * DECAY) - LEARN * corrected, moment, second)]
    unnamed x32 -> x22, local copies, waits for them, and re-layouts: 24.1 us -> 9.54 us
    gather x3 -> x0, local copies, waits for them, and re-layouts: 7 us -> none  [the longest x1 3.35 us: on_device(): source = all_rows // HD * HD + rotary_order[all_rows % HD]]
    sub x1 -> x0, local copies, waits for them, and re-layouts: 5.67 us -> none  [adam_update(): return (param * (1.0 - LEARN * DECAY) - LEARN * corrected, moment, second)]
  transfers between devices with their start and end apart: 4 -> 0, of which waited for: 3 -> 0; matrix products, arithmetic and copies ran while one was open for 19% -> 0% of each run, Pallas kernels for 0% -> 0%
where the time goes in v1:
time: 87.3 us; the launch traced here: 86.9 us
  Pallas kernels  76.7 us (88%)
  local copies, waits for them, and re-layouts  9.54 us (11%)
    pallas_call x1, Pallas kernels, on_device(): pl.pallas_call(functools.partial(kernel, n_dp, n_ex), out_shape=[shape(ex...  50.9 us
    pallas_call x1, Pallas kernels, on_device(): pl.pallas_call(functools.partial(place_slots, n_ex), out_shape=shape(arri...  25.8 us
    unnamed x22, local copies, waits for them, and re-layouts  9.54 us

profile of v1, /device:TPU:0, one launch (start us, length us, event | category | flops | bytes accessed | tf_op | source)
XLA Modules:
  0.0 86.9 jit_solution(4854279531687932344)
XLA Ops:
  0.6 1.4 %copy.20.e_scale = f32[4,12,16]{2,1,0:T(8,128)} copy(f32[4,12,16]{2,0,1:T(4,128)} %param.20) | data formatting | bytes 6144 | tf_op args[8]
  2.0 50.9 %reduce_update_exchange.1 = (f32[1,192,2048]{2,1,0:T(8,128)}, f32[1,192,2048]{2,1,0:T(8,128)}, f32[1,192,2048]{2,1,0:T(8,128)}, f32[64,1024]{1,0:T(8,128)}, f32[...) custom-call(f32[4,2,192,2048]{3,2,1,0:T(8,128)} %bitcast.4, ...), custom_call_target="tpu_custom_call" | custom-call | tf_op jit(solution)/shard_map/reduce_update_exchange/pallas_call | solution.py:425
  52.9 0.0 copy-start.2
  52.9 25.8 %place_slots.1 = bf16[4,192,512]{2,1,0:T(8,128)(2,1)} custom-call(s32[4]{0:T(128)} %slot.1, bf16[4,192,512]{2,1,0:T(8,128)(2,1)} %get-tuple-element.22.arrived), custom_call_target="tpu_custom_call" | custom-call | tf_op jit(solution)/shard_map/place_slots/pallas_call | solution.py:477
  78.7 0.0 copy-done.2
  78.7 0.0 copy-start.1
  78.7 1.1 %copy.28 = f32[1,192,2048]{2,1,0:T(8,128)} copy(f32[1,192,2048]{2,1,0:T(8,128)S(1)} %copy-done.2) | data formatting | bytes 3145728
  79.8 0.8 copy-done.1
  80.7 0.0 copy-start
  80.7 1.1 %copy.29 = f32[1,192,2048]{2,1,0:T(8,128)} copy(f32[1,192,2048]{2,1,0:T(8,128)S(1)} %copy-done.1) | data formatting | bytes 3145728
  81.8 0.8 copy-done
  82.6 0.0 copy-start.6
  82.6 0.0 copy-start.5
  82.6 0.0 copy-start.4
  82.6 1.1 %copy.30 = f32[1,192,2048]{2,1,0:T(8,128)} copy(f32[1,192,2048]{2,1,0:T(8,128)S(1)} %copy-done) | data formatting | bytes 3145728
  83.8 0.0 copy-done.6
  83.8 0.0 copy-start.3
  83.8 0.7 copy.31
  84.5 0.0 copy-done.5
  84.5 0.7 copy.32
  85.2 0.0 copy-done.4
  85.2 0.7 copy.33
  85.9 0.0 copy-done.3
  85.9 1.0 %copy.34 = bf16[1024,512]{1,0:T(8,128)(2,1)} copy(bf16[1024,512]{1,0:T(8,128)(2,1)S(1)} %copy-done.3) | data formatting | bytes 2097152
Async XLA Ops:
  52.9 25.8 %copy-start.2 = (f32[1,192,2048]{2,1,0:T(8,128)S(1)}, f32[1,192,2048]{2,1,0:T(8,128)}, u32[]{:S(2)}) copy-start(f32[1,192,2048]{2,1,0:T(8,128)} %get-tuple-element.32) | copy-start | bytes 4718596
  78.7 2.0 %copy-start.1 = (f32[1,192,2048]{2,1,0:T(8,128)S(1)}, f32[1,192,2048]{2,1,0:T(8,128)}, u32[]{:S(2)}) copy-start(f32[1,192,2048]{2,1,0:T(8,128)} %get-tuple-element.33) | copy-start | bytes 4718596
  80.7 2.0 %copy-start = (f32[1,192,2048]{2,1,0:T(8,128)S(1)}, f32[1,192,2048]{2,1,0:T(8,128)}, u32[]{:S(2)}) copy-start(f32[1,192,2048]{2,1,0:T(8,128)} %get-tuple-element.34) | copy-start | bytes 4718596
  82.6 1.2 %copy-start.6 = (f32[64,1024]{1,0:T(8,128)S(1)}, f32[64,1024]{1,0:T(8,128)}, u32[]{:S(2)}) copy-start(f32[64,1024]{1,0:T(8,128)} %get-tuple-element.35) | copy-start | bytes 786436
  82.6 1.9 %copy-start.5 = (f32[64,1024]{1,0:T(8,128)S(1)}, f32[64,1024]{1,0:T(8,128)}, u32[]{:S(2)}) copy-start(f32[64,1024]{1,0:T(8,128)} %get-tuple-element.36) | copy-start | bytes 786436
  82.6 2.6 %copy-start.4 = (f32[64,1024]{1,0:T(8,128)S(1)}, f32[64,1024]{1,0:T(8,128)}, u32[]{:S(2)}) copy-start(f32[64,1024]{1,0:T(8,128)} %get-tuple-element.37) | copy-start | bytes 786436
  83.8 2.1 %copy-start.3 = (bf16[1024,512]{1,0:T(8,128)(2,1)S(1)}, bf16[1024,512]{1,0:T(8,128)(2,1)}, u32[]{:S(2)}) copy-start(bf16[1024,512]{1,0:T(8,128)(2,1)} %get-tuple-element.39) | copy-start | bytes 3145732

commit v2 on v1

--- a/solution.py
+++ b/solution.py
@@ -39,6 +39,10 @@
     lax.fori_loop(0, count, step, 0)
 
 
+def parts_of(cw):
+    return max(1, cw // 512 * 2)
+
+
 def kernel(
     n_dp,
     n_ex,
@@ -50,9 +54,9 @@
     kp_hbm,
     km_hbm,
     ks_hbm,
-    e_scale,
-    k_scale,
-    order,
+    e_scale_hbm,
+    k_scale_hbm,
+    order_hbm,
     o_ep,
     o_em,
     o_es,
@@ -65,15 +69,15 @@
     e_own,
     e_s0s,
     e_s0r,
-    e_state,
     e_grid,
     k_far,
     k_own,
     k_s0s,
     k_s0r,
-    k_state,
     k_gath,
-    k_out,
+    e_scale,
+    k_scale,
+    order,
     *rest,
 ):
     chips = n_dp // 2
@@ -83,7 +87,7 @@
     e_rcv = [rest.pop(0) for _ in range(m)]
     k_snd = [rest.pop(0) for _ in range(m)]
     k_rcv = [rest.pop(0) for _ in range(m)]
-    load_sem, s0_sem, rs_sem, out_sem, a2a_sem, ag_sem, pair_sem, key_sem = rest
+    load_sem, s0_sem, rs_sem, a2a_sem, ag_sem, pair_sem, small_sem = rest
 
     d = lax.axis_index("dp")
     z = lax.axis_index("expert")
@@ -106,15 +110,18 @@
     rows, width = ep_hbm.shape[1:]
     krows, kwidth = kp_hbm.shape
     cw = width // n_ex
+    parts = parts_of(cw)
+    uw = cw // parts
+    n_units = n_ex * parts
 
     def place(t):
-        return (z + n_ex - 1 - t) % n_ex
+        return (z + n_ex - 1 - t // parts) % n_ex
 
     class Unit:
         pass
 
     units = []
-    for u in range(n_ex + 1):
+    for u in range(n_units + 1):
         w = Unit()
         w.u = u
         if u == 0:
@@ -123,21 +130,20 @@
             w.far, w.own, w.s0s, w.s0r = k_far, k_own, k_s0s, k_s0r
             w.snd, w.rcv = k_snd, k_rcv
             w.grad = kg_hbm
-            w.state = [k_state.at[i] for i in range(3)]
+            w.state = [o_kp, o_km, o_ks]
             w.state_in = [kp_hbm, km_hbm, ks_hbm]
-            w.state_out = [o_kp, o_km, o_ks]
         else:
             t = u - 1
             w.dest = place(t)
-            w.rows, w.cols = rows, cw
-            w.columns = pl.ds(pl.multiple_of(w.dest * cw, cw), cw)
+            w.rows, w.cols = rows, uw
+            w.at = t % parts * uw
+            w.columns = pl.ds(pl.multiple_of(w.dest * cw + w.at, uw), uw)
             w.far, w.own, w.s0s, w.s0r = (r.at[t] for r in (e_far, e_own, e_s0s, e_s0r))
             w.snd = [r.at[t] for r in e_snd]
             w.rcv = [r.at[t] for r in e_rcv]
             w.grad = eg_hbm
-            w.state = [e_state.at[t, i] for i in range(3)]
+            w.state = [r.at[0, :, w.columns] for r in (o_ep, o_em, o_es)]
             w.state_in = [r.at[0, :, w.columns] for r in (ep_hbm, em_hbm, es_hbm)]
-            w.state_out = [r.at[0, :, w.columns] for r in (o_ep, o_em, o_es)]
         w.half = w.cols // 2
         w.load_far = pltpu.make_async_copy(
             w.grad.at[:, 1 - core, :, w.columns], w.far, load_sem.at[u, 0]
@@ -147,10 +153,6 @@
         )
         w.load_state = [
             pltpu.make_async_copy(w.state_in[i], w.state[i], load_sem.at[u, 2 + i])
-            for i in range(3)
-        ]
-        w.store_state = [
-            pltpu.make_async_copy(w.state[i], w.state_out[i], out_sem.at[u, i])
             for i in range(3)
         ]
         w.s0 = pltpu.make_async_remote_copy(
@@ -177,9 +179,18 @@
         ]
         units.append(w)
 
+    small = [
+        pltpu.make_async_copy(source, target, small_sem.at[i])
+        for i, (source, target) in enumerate(
+            ((k_scale_hbm, k_scale), (e_scale_hbm, e_scale), (order_hbm, order))
+        )
+    ]
     for w in units:
         w.load_far.start()
         w.load_own.start()
+        if w.u == 0:
+            for c in small:
+                c.start()
     for w in units:
         for c in w.load_state:
             c.start()
@@ -243,6 +254,9 @@
     def update(w):
         for c in w.load_state:
             c.wait()
+        if w.u == 0:
+            for c in small:
+                c.wait()
         step = math.gcd(w.rows, 8192 // w.half)
         for h in range(2):
             w.rs[m - 1][h].wait_recv()
@@ -260,29 +274,28 @@
                     if w.u == 0:
                         scale = k_scale[block, at]
                     else:
-                        scale = e_scale[z, block, w.dest * (cw // BLOCK) + at]
+                        scale = e_scale[block, z, w.dest * (cw // BLOCK) + w.at // BLOCK + at]
                     part = new[0][:, j * BLOCK : (j + 1) * BLOCK] / scale
                     part = jnp.clip(part, -LIMIT, LIMIT)
                     cols = slice(at * BLOCK, (at + 1) * BLOCK)
                     if w.u == 0:
                         k_gath[chip, core, r, cols] = part.astype(BF16)
+                    elif w.u <= n_units - parts:
+                        e_grid[w.u - 1, r, cols] = part.astype(BF16)
                     else:
-                        e_grid[w.u - 1, r, cols] = part.astype(BF16)
+                        lane = w.at + at * BLOCK
+                        o_arr[z, r, lane : lane + BLOCK] = part.astype(BF16)
 
             loop(w.rows // step, body)
-        for c in w.store_state:
-            c.start()
         if w.u == 0:
             gather_send(0)
-        else:
+        elif w.u <= n_units - parts:
             a2a(w.u - 1).start()
 
     def a2a(t):
-        if t == n_ex - 1:
-            return pltpu.make_async_copy(e_grid.at[t], o_arr.at[z], a2a_sem.at[t, 0])
         return pltpu.make_async_remote_copy(
             src_ref=e_grid.at[t],
-            dst_ref=o_arr.at[z],
+            dst_ref=o_arr.at[z, :, pl.ds(t % parts * uw, uw)],
             send_sem=a2a_sem.at[t, 0],
             recv_sem=a2a_sem.at[t, 1],
             device_id=(d, place(t)),
@@ -320,7 +333,6 @@
         device_id=(other_core, z),
         device_id_type=MESH,
     )
-    store_key = pltpu.make_async_copy(k_out, o_key, key_sem.at[0])
 
     def gather_send(s):
         for c in gather_copies(s):
@@ -340,51 +352,48 @@
         pick = jnp.where(source == order[...], 1.0, 0.0).astype(BF16)
         span = HD // (2 * krows)
         wide = 256
-        for head in range(k_out.shape[1] // HD):
+        for head in range(o_key.shape[1] // HD):
             for j in range(kwidth // wide):
                 cols = slice(j * wide, (j + 1) * wide)
                 block = k_gath[head * span : (head + 1) * span, :, :, cols].reshape(HD, wide)
                 turned = lax.dot_general(
                     block, pick, (((0,), (0,)), ((), ())), preferred_element_type=F32
                 )
-                k_out[cols, head * HD : (head + 1) * HD] = turned.astype(BF16)
-        store_key.start()
+                o_key[cols, head * HD : (head + 1) * HD] = turned.astype(BF16)
 
     stages = [first] + [functools.partial(reduce, s=s) for s in range(m)] + [update]
     extra = [functools.partial(gather_next, s) for s in range(m)] + [key_finish]
-    for slot in range(len(units) + len(stages) - 1):
-        for s, stage in enumerate(stages):
-            if 0 <= slot - s < len(units):
-                stage(units[slot - s])
-        if 0 <= slot - len(stages) < len(extra):
-            extra[slot - len(stages)]()
-    for task in extra[len(units) - 1 :]:
-        task()
-
-    for t in range(n_ex):
-        if t == n_ex - 1:
-            a2a(t).wait()
-        else:
-            a2a(t).wait_send()
-            a2a(t).wait_recv()
+    lags = [0, 1] + [1 + 2 * s for s in range(1, m + 1)]
+    for slot in range(len(units) + lags[-1]):
+        for stage, lag in zip(stages, lags):
+            if 0 <= slot - lag < len(units):
+                stage(units[slot - lag])
+        if 0 <= slot - lags[-1] - 1 < len(extra):
+            extra[slot - lags[-1] - 1]()
+
+    for t in range(n_units - parts):
+        a2a(t).wait_send()
+        a2a(t).wait_recv()
     for w in units:
         w.s0.wait_send()
         for s in range(m):
             for h in range(2):
                 w.rs[s][h].wait_send()
-        for c in w.store_state:
-            c.wait()
     for s in range(m):
         for c in gather_copies(s):
             c.wait_send()
     pair.wait_send()
-    store_key.wait()
-
-
-def place_slots(n_ex, slot, arrived, placed, sems):
-    copies = [
-        pltpu.make_async_copy(arrived.at[e], placed.at[slot[e]], sems.at[e]) for e in range(n_ex)
-    ]
+
+
+def finish(n_ex, slot, *refs):
+    sources, targets, sems = refs[:8], refs[8:16], refs[16]
+    copies = []
+    for i in (0, 1, 2, 7, 3, 4, 5):
+        copies.append(pltpu.make_async_copy(sources[i], targets[i], sems.at[i]))
+    for e in range(n_ex):
+        copies.append(
+            pltpu.make_async_copy(sources[6].at[e], targets[6].at[slot[e]], sems.at[8 + e])
+        )
     for c in copies:
         c.start()
     for c in copies:
@@ -414,10 +423,13 @@
         krows, kwidth = key_param.shape
         key_rows = key_partials.shape[1]
         cw = width // n_ex
+        parts = parts_of(cw)
+        n_units, uw = n_ex * parts, cw // parts
         eg = expert_partials.reshape(chips, 2, rows, width)
         kg = key_partials.reshape(chips, 2, krows, kwidth)
         shape = jax.ShapeDtypeStruct
         anywhere = pl.BlockSpec(memory_space=pl.ANY)
+        hbm = pl.BlockSpec(memory_space=pltpu.HBM)
         scalars = pl.BlockSpec(memory_space=pltpu.SMEM)
         vector = pl.BlockSpec(memory_space=pltpu.VMEM)
         dma = pltpu.SemaphoreType.DMA
@@ -427,37 +439,36 @@
             out_shape=[shape(expert_param.shape, F32)] * 3
             + [shape(key_param.shape, F32)] * 3
             + [shape((n_ex, rows, cw), BF16), shape((kwidth, key_rows), BF16)],
-            in_specs=[anywhere] * 8 + [scalars] * 2 + [vector],
-            out_specs=[anywhere] * 8,
+            in_specs=[hbm] * 11,
+            out_specs=[vector] * 8,
             scratch_shapes=[
-                pltpu.VMEM((n_ex, chips, rows, cw), F32),
-                pltpu.VMEM((n_ex, chips, rows, cw), F32),
-                pltpu.VMEM((n_ex, chips, rows, cw), BF16),
-                pltpu.VMEM((n_ex, chips, rows, cw), BF16),
-                pltpu.VMEM((n_ex, 3, rows, cw), F32),
-                pltpu.VMEM((n_ex, rows, cw), BF16),
+                pltpu.VMEM((n_units, chips, rows, uw), F32),
+                pltpu.VMEM((n_units, chips, rows, uw), F32),
+                pltpu.VMEM((n_units, chips, rows, uw), BF16),
+                pltpu.VMEM((n_units, chips, rows, uw), BF16),
+                pltpu.VMEM((n_units - parts, rows, uw), BF16),
                 pltpu.VMEM((chips, krows, kwidth), F32),
                 pltpu.VMEM((chips, krows, kwidth), F32),
                 pltpu.VMEM((chips, krows, kwidth), BF16),
                 pltpu.VMEM((chips, krows, kwidth), BF16),
-                pltpu.VMEM((3, krows, kwidth), F32),
                 pltpu.VMEM((chips, 2, krows, kwidth), BF16),
-                pltpu.VMEM((kwidth, key_rows), BF16),
+                pltpu.SMEM(expert_scales.shape[1:2] + (n_ex,) + expert_scales.shape[2:], F32),
+                pltpu.SMEM(key_scales.shape, F32),
+                pltpu.VMEM((1, HD), jnp.int32),
             ]
-            + [pltpu.VMEM((n_ex, 2, c, rows, cw // 2), BF16) for c in counts] * 2
+            + [pltpu.VMEM((n_units, 2, c, rows, uw // 2), BF16) for c in counts] * 2
             + [pltpu.VMEM((2, c, krows, kwidth // 2), BF16) for c in counts] * 2
             + [
-                dma((n_ex + 1, 5)),
-                dma((n_ex + 1, 2)),
-                dma((n_ex + 1, m, 2, 2)),
-                dma((n_ex + 1, 3)),
-                dma((n_ex, 2)),
+                dma((n_units + 1, 5)),
+                dma((n_units + 1, 2)),
+                dma((n_units + 1, m, 2, 2)),
+                dma((n_units - parts, 2)),
                 dma((m, 2, 2 ** (m - 1), 2)),
                 dma((2,)),
-                dma((1,)),
+                dma((3,)),
             ],
             compiler_params=pltpu.CompilerParams(
-                collective_id=0, has_side_effects=True, vmem_limit_bytes=58 * 2**20
+                collective_id=0, has_side_effects=True, vmem_limit_bytes=int(46 * 2**20)
             ),
             name="reduce_update_exchange",
         )(
@@ -469,21 +480,20 @@
             key_param,
             key_moment,
             key_second,
-            expert_scales,
+            jnp.transpose(expert_scales, (1, 0, 2)),
             key_scales,
             rotary_order.reshape(1, HD),
         )
-        new_ep, new_em, new_es, new_kp, new_km, new_ks, arrived, server_key = out
-        placed = pl.pallas_call(
-            functools.partial(place_slots, n_ex),
-            out_shape=shape(arrived.shape, BF16),
-            in_specs=[scalars, anywhere],
-            out_specs=anywhere,
-            scratch_shapes=[dma((n_ex,))],
-            name="place_slots",
-        )(expert_slot, arrived)
-        server_expert = jnp.transpose(placed, (0, 2, 1))
-        return (new_ep, new_em, new_es, new_kp, new_km, new_ks, server_expert, server_key)
+        *state, placed, server_key = pl.pallas_call(
+            functools.partial(finish, n_ex),
+            out_shape=[shape(x.shape, x.dtype) for x in out],
+            in_specs=[scalars] + [vector] * 8,
+            out_specs=[anywhere] * 8,
+            scratch_shapes=[dma((8 + n_ex,))],
+            compiler_params=pltpu.CompilerParams(vmem_limit_bytes=16 * 2**20),
+            name="finish",
+        )(expert_slot, *out)
+        return (*state, jnp.transpose(placed, (0, 2, 1)), server_key)
 
     return jax.shard_map(
         on_device,

time: 87.3 us -> 57.9 us (0.66)
  Pallas kernels: 76.7 us -> 52 us
  local copies, waits for them, and re-layouts: 9.54 us -> 4.92 us
    pallas_call x1, Pallas kernels: 25.8 us -> 3.61 us  [on_device(): pl.pallas_call(functools.partial(finish, n_ex), out_shape=[shape(x.shape,...]
    unnamed x22 -> x14, local copies, waits for them, and re-layouts: 9.54 us -> 4.92 us
    pallas_call x1, Pallas kernels: 50.9 us -> 48.4 us  [on_device(): pl.pallas_call(functools.partial(kernel, n_dp, n_ex), out_shape=[shape(ex...]
where the time goes in v2:
time: 57.9 us; the launch traced here: 57.6 us
  Pallas kernels  52 us (90%)
  local copies, waits for them, and re-layouts  4.92 us (8%)
  between operations  0.67 us (1%)
    pallas_call x1, Pallas kernels, on_device(): pl.pallas_call(functools.partial(kernel, n_dp, n_ex), out_shape=[shape(ex...  48.4 us
    unnamed x14, local copies, waits for them, and re-layouts  4.92 us
    pallas_call x1, Pallas kernels, on_device(): pl.pallas_call(functools.partial(finish, n_ex), out_shape=[shape(x.shape,...  3.61 us

profile of v2, /device:TPU:0, one launch (start us, length us, event | category | flops | bytes accessed | tf_op | source)
XLA Modules:
  0.0 57.6 jit_solution(1867494588587163785)
XLA Ops:
  0.6 0.0 copy-start
  0.6 0.9 %copy-done = f32[64,1024]{1,0:T(8,128)S(1)} copy-done((f32[64,1024]{1,0:T(8,128)S(1)}, f32[64,1024]{1,0:T(8,128)}, u32[]{:S(2)}) %copy-start) | copy-done | bytes 262168
  1.6 0.0 copy-start.1
  1.6 0.9 %copy-done.1 = f32[64,1024]{1,0:T(8,128)S(1)} copy-done((f32[64,1024]{1,0:T(8,128)S(1)}, f32[64,1024]{1,0:T(8,128)}, u32[]{:S(2)}) %copy-start.1) | copy-done | bytes 262168
  2.5 0.0 copy-start.2
  2.5 0.9 %copy-done.2 = f32[64,1024]{1,0:T(8,128)S(1)} copy-done((f32[64,1024]{1,0:T(8,128)S(1)}, f32[64,1024]{1,0:T(8,128)}, u32[]{:S(2)}) %copy-start.2) | copy-done | bytes 262168
  3.5 0.0 copy-start.3
  3.5 0.7 %copy-done.3 = f32[4,12,16]{2,0,1:T(4,128)S(1)} copy-done((f32[4,12,16]{2,0,1:T(4,128)S(1)}, f32[4,12,16]{2,0,1:T(4,128)}, u32[]{:S(2)}) %copy-start.3) | copy-done | bytes 3096
  4.2 0.0 copy-start.4
  4.2 0.7 %copy-done.4 = f32[4,8]{1,0:T(4,128)S(1)} copy-done((f32[4,8]{1,0:T(4,128)S(1)}, f32[4,8]{1,0:T(4,128)}, u32[]{:S(2)}) %copy-start.4) | copy-done | bytes 152
  4.9 0.0 copy-start.5
  4.9 0.7 %copy-done.5 = s32[128]{0:T(128)S(1)} copy-done((s32[128]{0:T(128)S(1)}, s32[128]{0:T(128)}, u32[]{:S(2)}) %copy-start.5) | copy-done | bytes 536
  5.6 0.0 copy-start.6
  5.6 48.4 %reduce_update_exchange.1 = (f32[1,192,2048]{2,1,0:T(8,128)S(1)}, f32[1,192,2048]{2,1,0:T(8,128)S(1)}, f32[1,192,2048]{2,1,0:T(8,128)S(1)}, f32[64,1024]{1,0:T(8...) custom-call(f32[4,2,192,2048]{3,2,1,0:T(8,128)} %bitcast.7, ...), custom_call_target="tpu_custom_call" | custom-call | tf_op jit(solution)/shard_map/reduce_update_exchange/pallas_call | solution.py:437
  54.0 0.0 copy-done.6
  54.0 3.6 %finish.1 = (f32[1,192,2048]{2,1,0:T(8,128)}, f32[1,192,2048]{2,1,0:T(8,128)}, f32[1,192,2048]{2,1,0:T(8,128)}, f32[64,1024]{1,0:T(8,128)}, f32[64,1024]{1,0:T(8...) custom-call(s32[4]{0:T(128)S(1)} %copy-done.6, ...), custom_call_target="tpu_custom_call" | custom-call | tf_op jit(solution)/shard_map/finish/pallas_call | solution.py:487
Async XLA Ops:
  0.6 1.0 %copy-start = (f32[64,1024]{1,0:T(8,128)S(1)}, f32[64,1024]{1,0:T(8,128)}, u32[]{:S(2)}) copy-start(f32[64,1024]{1,0:T(8,128)} %kp_hbm.1) | copy-start | bytes 786436
  1.6 0.9 %copy-start.1 = (f32[64,1024]{1,0:T(8,128)S(1)}, f32[64,1024]{1,0:T(8,128)}, u32[]{:S(2)}) copy-start(f32[64,1024]{1,0:T(8,128)} %km_hbm.1) | copy-start | bytes 786436
  2.5 0.9 %copy-start.2 = (f32[64,1024]{1,0:T(8,128)S(1)}, f32[64,1024]{1,0:T(8,128)}, u32[]{:S(2)}) copy-start(f32[64,1024]{1,0:T(8,128)} %ks_hbm.1) | copy-start | bytes 786436
  3.5 0.7 %copy-start.3 = (f32[4,12,16]{2,0,1:T(4,128)S(1)}, f32[4,12,16]{2,0,1:T(4,128)}, u32[]{:S(2)}) copy-start(f32[4,12,16]{2,0,1:T(4,128)} %param.20) | copy-start | bytes 9220
  4.2 0.7 %copy-start.4 = (f32[4,8]{1,0:T(4,128)S(1)}, f32[4,8]{1,0:T(4,128)}, u32[]{:S(2)}) copy-start(f32[4,8]{1,0:T(4,128)} %k_scale_hbm.1) | copy-start | bytes 388
  4.9 0.7 %copy-start.5 = (s32[128]{0:T(128)S(1)}, s32[128]{0:T(128)}, u32[]{:S(2)}) copy-start(s32[128]{0:T(128)} %param.22) | copy-start | bytes 1540
  5.6 48.4 %copy-start.6 = (s32[4]{0:T(128)S(1)}, s32[4]{0:T(128)}, u32[]{:S(2)}) copy-start(s32[4]{0:T(128)} %slot.1) | copy-start | bytes 52

commit v3 on v2

--- a/solution.py
+++ b/solution.py
@@ -185,22 +185,23 @@
             ((k_scale_hbm, k_scale), (e_scale_hbm, e_scale), (order_hbm, order))
         )
     ]
-    for w in units:
-        w.load_far.start()
-        w.load_own.start()
-        if w.u == 0:
-            for c in small:
+    def load(u):
+        if 0 <= u < len(units):
+            units[u].load_far.start()
+            units[u].load_own.start()
+
+    def load_state(u):
+        if 0 <= u < len(units):
+            for c in units[u].load_state:
                 c.start()
-    for w in units:
-        for c in w.load_state:
-            c.start()
 
     barrier = pltpu.get_barrier_semaphore()
     peers = [(other_core, z)] + [(partner(i), z) for i in range(m)]
     peers += [(d, (z + k) % n_ex) for k in range(1, n_ex)]
     for peer in peers:
         pl.semaphore_signal(barrier, inc=1, device_id=peer, device_id_type=MESH)
-    pl.semaphore_wait(barrier, len(peers))
+    load(0)
+    load(1)
 
     def index_in(values, h, s):
         total = 0
@@ -227,6 +228,8 @@
             w.s0s[q, r, :] = w.far[q, r, :].astype(BF16)
 
         loop(chips * per, body)
+        if w.u == 0:
+            pl.semaphore_wait(barrier, len(peers))
         w.s0.start()
 
     def reduce(w, s):
@@ -291,6 +294,10 @@
             gather_send(0)
         elif w.u <= n_units - parts:
             a2a(w.u - 1).start()
+        w.s0.wait_send()
+        for s in range(m):
+            for h in range(2):
+                w.rs[s][h].wait_send()
 
     def a2a(t):
         return pltpu.make_async_remote_copy(
@@ -362,23 +369,27 @@
                 o_key[cols, head * HD : (head + 1) * HD] = turned.astype(BF16)
 
     stages = [first] + [functools.partial(reduce, s=s) for s in range(m)] + [update]
-    extra = [functools.partial(gather_next, s) for s in range(m)] + [key_finish]
-    lags = [0, 1] + [1 + 2 * s for s in range(1, m + 1)]
+    lags = [0, 1] + [1 + 2 * s for s in range(1, m)] + [2 * m]
+    last = len(units) - 1
     for slot in range(len(units) + lags[-1]):
-        for stage, lag in zip(stages, lags):
-            if 0 <= slot - lag < len(units):
+        for s, (stage, lag) in enumerate(zip(stages, lags)):
+            if 0 <= slot - lag <= last:
                 stage(units[slot - lag])
-        if 0 <= slot - lags[-1] - 1 < len(extra):
-            extra[slot - lags[-1] - 1]()
+            if s == 0:
+                load(slot + 2)
+                load_state(slot)
+                if slot == 0:
+                    for c in small:
+                        c.start()
+            if s == m and slot - lag == last - 1:
+                key_finish()
+        step = slot - lags[-1] - 1
+        if 0 <= step < m:
+            gather_next(step)
 
     for t in range(n_units - parts):
         a2a(t).wait_send()
         a2a(t).wait_recv()
-    for w in units:
-        w.s0.wait_send()
-        for s in range(m):
-            for h in range(2):
-                w.rs[s][h].wait_send()
     for s in range(m):
         for c in gather_copies(s):
             c.wait_send()
@@ -434,6 +445,7 @@
         vector = pl.BlockSpec(memory_space=pltpu.VMEM)
         dma = pltpu.SemaphoreType.DMA
         counts = [2 ** (m - 1 - s) for s in range(m)]
+        here = functools.partial(pltpu.with_memory_space_constraint, memory_space=pltpu.HBM)
         out = pl.pallas_call(
             functools.partial(kernel, n_dp, n_ex),
             out_shape=[shape(expert_param.shape, F32)] * 3
@@ -472,17 +484,22 @@
             ),
             name="reduce_update_exchange",
         )(
-            eg,
-            kg,
-            expert_param,
-            expert_moment,
-            expert_second,
-            key_param,
-            key_moment,
-            key_second,
-            jnp.transpose(expert_scales, (1, 0, 2)),
-            key_scales,
-            rotary_order.reshape(1, HD),
+            *map(
+                here,
+                (
+                    eg,
+                    kg,
+                    expert_param,
+                    expert_moment,
+                    expert_second,
+                    key_param,
+                    key_moment,
+                    key_second,
+                    jnp.transpose(expert_scales, (1, 0, 2)),
+                    key_scales,
+                    rotary_order.reshape(1, HD),
+                ),
+            )
         )
         *state, placed, server_key = pl.pallas_call(
             functools.partial(finish, n_ex),

time: 57.9 us -> 51.9 us (0.90)
  local copies, waits for them, and re-layouts: 4.92 us -> 0.01 us
  Pallas kernels: 52 us -> 51.1 us
    unnamed x14 -> x2, local copies, waits for them, and re-layouts: 4.92 us -> 0.01 us
    pallas_call x1, Pallas kernels: 48.4 us -> 47.5 us  [on_device(): pl.pallas_call(functools.partial(kernel, n_dp, n_ex), out_shape=[shape(ex...]
where the time goes in v3:
time: 51.9 us; the launch traced here: 51.8 us
  Pallas kernels  51.1 us (98%)
  between operations  0.66 us (1%)
    pallas_call x1, Pallas kernels, on_device(): pl.pallas_call(functools.partial(kernel, n_dp, n_ex), out_shape=[shape(ex...  47.5 us
    pallas_call x1, Pallas kernels, on_device(): pl.pallas_call(functools.partial(finish, n_ex), out_shape=[shape(x.shape,...  3.61 us

profile of v3, /device:TPU:0, one launch (start us, length us, event | category | flops | bytes accessed | tf_op | source)
XLA Modules:
  0.0 51.8 jit_solution(6329507326021505100)
XLA Ops:
  0.6 0.0 copy-start
  0.6 47.5 %reduce_update_exchange.1 = (f32[1,192,2048]{2,1,0:T(8,128)S(1)}, f32[1,192,2048]{2,1,0:T(8,128)S(1)}, f32[1,192,2048]{2,1,0:T(8,128)S(1)}, f32[64,1024]{1,0:T(8...) custom-call(f32[4,2,192,2048]{3,2,1,0:T(8,128)} %bitcast.5, ...), custom_call_target="tpu_custom_call" | custom-call | tf_op jit(solution)/shard_map/reduce_update_exchange/pallas_call | solution.py:449
  48.2 0.0 copy-done
  48.2 3.6 %finish.1 = (f32[1,192,2048]{2,1,0:T(8,128)}, f32[1,192,2048]{2,1,0:T(8,128)}, f32[1,192,2048]{2,1,0:T(8,128)}, f32[64,1024]{1,0:T(8,128)}, f32[64,1024]{1,0:T(8...) custom-call(s32[4]{0:T(128)S(1)} %copy-done, ...), custom_call_target="tpu_custom_call" | custom-call | tf_op jit(solution)/shard_map/finish/pallas_call | solution.py:504
Async XLA Ops:
  0.6 47.5 %copy-start = (s32[4]{0:T(128)S(1)}, s32[4]{0:T(128)}, u32[]{:S(2)}) copy-start(s32[4]{0:T(128)} %slot.1) | copy-start | bytes 52

commit v4 on v3

--- a/solution.py
+++ b/solution.py
@@ -39,8 +39,21 @@
     lax.fori_loop(0, count, step, 0)
 
 
-def parts_of(cw):
-    return max(1, cw // 512 * 2)
+def plan(n_ex, cw):
+    units = []
+    for t in range(n_ex):
+        wide = min(cw, 2 * BLOCK)
+        sizes = [wide] * (cw // wide)
+        if wide > BLOCK and t == 0:
+            sizes[:1] = [BLOCK, wide - BLOCK]
+        if wide > BLOCK and t == n_ex - 1:
+            sizes[-1:] = [wide - BLOCK, BLOCK]
+        at = 0
+        for size in sizes:
+            units.append((t, at, size))
+            at += size
+    units.insert(2, None)
+    return units
 
 
 def kernel(
@@ -65,15 +78,6 @@
     o_ks,
     o_arr,
     o_key,
-    e_far,
-    e_own,
-    e_s0s,
-    e_s0r,
-    e_grid,
-    k_far,
-    k_own,
-    k_s0s,
-    k_s0r,
     k_gath,
     e_scale,
     k_scale,
@@ -82,12 +86,8 @@
 ):
     chips = n_dp // 2
     m = chips.bit_length() - 1
-    rest = list(rest)
-    e_snd = [rest.pop(0) for _ in range(m)]
-    e_rcv = [rest.pop(0) for _ in range(m)]
-    k_snd = [rest.pop(0) for _ in range(m)]
-    k_rcv = [rest.pop(0) for _ in range(m)]
-    load_sem, s0_sem, rs_sem, a2a_sem, ag_sem, pair_sem, small_sem = rest
+    load_sem, s0_sem, rs_sem, a2a_sem, ag_sem, pair_sem, small_sem = rest[:7]
+    rest = list(rest[7:])
 
     d = lax.axis_index("dp")
     z = lax.axis_index("expert")
@@ -110,41 +110,45 @@
     rows, width = ep_hbm.shape[1:]
     krows, kwidth = kp_hbm.shape
     cw = width // n_ex
-    parts = parts_of(cw)
-    uw = cw // parts
-    n_units = n_ex * parts
-
-    def place(t):
-        return (z + n_ex - 1 - t // parts) % n_ex
+    layout = plan(n_ex, cw)
 
     class Unit:
         pass
 
     units = []
-    for u in range(n_units + 1):
+    for u, entry in enumerate(layout):
         w = Unit()
         w.u = u
-        if u == 0:
+        w.key = entry is None
+        w.far, w.own, w.s0s, w.s0r = (rest.pop(0) for _ in range(4))
+        w.snd = [rest.pop(0) for _ in range(m)]
+        w.rcv = [rest.pop(0) for _ in range(m)]
+        if w.key:
             w.rows, w.cols = krows, kwidth
             w.columns = pl.ds(0, kwidth)
-            w.far, w.own, w.s0s, w.s0r = k_far, k_own, k_s0s, k_s0r
-            w.snd, w.rcv = k_snd, k_rcv
             w.grad = kg_hbm
             w.state = [o_kp, o_km, o_ks]
             w.state_in = [kp_hbm, km_hbm, ks_hbm]
         else:
-            t = u - 1
-            w.dest = place(t)
-            w.rows, w.cols = rows, uw
-            w.at = t % parts * uw
-            w.columns = pl.ds(pl.multiple_of(w.dest * cw + w.at, uw), uw)
-            w.far, w.own, w.s0s, w.s0r = (r.at[t] for r in (e_far, e_own, e_s0s, e_s0r))
-            w.snd = [r.at[t] for r in e_snd]
-            w.rcv = [r.at[t] for r in e_rcv]
+            t, w.at, w.cols = entry
+            w.rows = rows
+            w.dest = (z + n_ex - 1 - t) % n_ex
+            w.mine = t == n_ex - 1
+            w.columns = pl.ds(pl.multiple_of(w.dest * cw + w.at, BLOCK), w.cols)
             w.grad = eg_hbm
             w.state = [r.at[0, :, w.columns] for r in (o_ep, o_em, o_es)]
             w.state_in = [r.at[0, :, w.columns] for r in (ep_hbm, em_hbm, es_hbm)]
-        w.half = w.cols // 2
+            if not w.mine:
+                w.grid = rest.pop(0)
+                w.exchange = pltpu.make_async_remote_copy(
+                    src_ref=w.grid,
+                    dst_ref=o_arr.at[z, :, pl.ds(w.at, w.cols)],
+                    send_sem=a2a_sem.at[u, 0],
+                    recv_sem=a2a_sem.at[u, 1],
+                    device_id=(d, w.dest),
+                    device_id_type=MESH,
+                )
+        w.half = w.rows // 2
         w.load_far = pltpu.make_async_copy(
             w.grad.at[:, 1 - core, :, w.columns], w.far, load_sem.at[u, 0]
         )
@@ -209,10 +213,16 @@
             total = total + values[b] * 2**k
         return total
 
-    def block_sum(w, values, h, s, r):
+    def rows_at(i, step):
+        return pl.ds(pl.multiple_of(i * step, step), step)
+
+    def rows_in(w, h, i, step):
+        return pl.ds(pl.multiple_of(h * w.half + i * step, step), step)
+
+    def block_sum(w, values, h, s, i, step):
         q = chip_of(values)
-        lanes = slice(h * w.half, (h + 1) * w.half)
-        total = w.own[q, r, lanes] + w.s0r[q, r, lanes].astype(F32)
+        r, whole = rows_at(i, step), rows_in(w, h, i, step)
+        total = w.own[q, whole, :] + w.s0r[q, whole, :].astype(F32)
         for past in range(s):
             total = total + w.rcv[past][h, index_in(values, h, past), r, :].astype(F32)
         return total
@@ -236,7 +246,7 @@
         if s == 0:
             w.load_own.wait()
             w.s0.wait_recv()
-        step = math.gcd(w.rows, 16384 // w.half)
+        step = math.gcd(w.half, 16384 // w.cols)
         for h in range(2):
             if s > 0:
                 w.rs[s - 1][h].wait_recv()
@@ -248,10 +258,10 @@
                     values[b] = (slot >> k) & 1
 
                 def body(i):
-                    r = pl.ds(pl.multiple_of(i * step, step), step)
-                    w.snd[s][h, slot, r, :] = block_sum(w, values, h, s, r).astype(BF16)
-
-                loop(w.rows // step, body)
+                    total = block_sum(w, values, h, s, i, step)
+                    w.snd[s][h, slot, rows_at(i, step), :] = total.astype(BF16)
+
+                loop(w.half // step, body)
             w.rs[s][h].start()
 
     def update(w):
@@ -260,54 +270,40 @@
         if w.u == 0:
             for c in small:
                 c.wait()
-        step = math.gcd(w.rows, 8192 // w.half)
+        step = math.gcd(w.half, max(16, 8192 // w.cols))
         for h in range(2):
             w.rs[m - 1][h].wait_recv()
 
             def body(i):
-                r = pl.ds(pl.multiple_of(i * step, step), step)
-                lanes = slice(h * w.half, (h + 1) * w.half)
-                grad = block_sum(w, bits, h, m, r)
-                new = adam_update(*(ref[r, lanes] for ref in w.state), grad)
+                r = rows_in(w, h, i, step)
+                grad = block_sum(w, bits, h, m, i, step)
+                new = adam_update(*(ref[r, :] for ref in w.state), grad)
                 for ref, value in zip(w.state, new):
-                    ref[r, lanes] = value
-                block = (d * w.rows + i * step) // BLOCK
-                for j in range(w.half // BLOCK):
-                    at = h * (w.half // BLOCK) + j
-                    if w.u == 0:
-                        scale = k_scale[block, at]
+                    ref[r, :] = value
+                block = (d * w.rows + h * w.half + i * step) // BLOCK
+                for j in range(w.cols // BLOCK):
+                    if w.key:
+                        scale = k_scale[block, j]
                     else:
-                        scale = e_scale[block, z, w.dest * (cw // BLOCK) + w.at // BLOCK + at]
-                    part = new[0][:, j * BLOCK : (j + 1) * BLOCK] / scale
-                    part = jnp.clip(part, -LIMIT, LIMIT)
-                    cols = slice(at * BLOCK, (at + 1) * BLOCK)
-                    if w.u == 0:
-                        k_gath[chip, core, r, cols] = part.astype(BF16)
-                    elif w.u <= n_units - parts:
-                        e_grid[w.u - 1, r, cols] = part.astype(BF16)
+                        scale = e_scale[block, z, w.dest * (cw // BLOCK) + w.at // BLOCK + j]
+                    cols = slice(j * BLOCK, (j + 1) * BLOCK)
+                    part = jnp.clip(new[0][:, cols] / scale, -LIMIT, LIMIT).astype(BF16)
+                    if w.key:
+                        k_gath[chip, core, r, cols] = part
+                    elif w.mine:
+                        o_arr[z, r, w.at + j * BLOCK : w.at + (j + 1) * BLOCK] = part
                     else:
-                        lane = w.at + at * BLOCK
-                        o_arr[z, r, lane : lane + BLOCK] = part.astype(BF16)
-
-            loop(w.rows // step, body)
-        if w.u == 0:
+                        w.grid[r, cols] = part
+
+            loop(w.half // step, body)
+        if w.key:
             gather_send(0)
-        elif w.u <= n_units - parts:
-            a2a(w.u - 1).start()
+        elif not w.mine:
+            w.exchange.start()
         w.s0.wait_send()
         for s in range(m):
             for h in range(2):
                 w.rs[s][h].wait_send()
-
-    def a2a(t):
-        return pltpu.make_async_remote_copy(
-            src_ref=e_grid.at[t],
-            dst_ref=o_arr.at[z, :, pl.ds(t % parts * uw, uw)],
-            send_sem=a2a_sem.at[t, 0],
-            recv_sem=a2a_sem.at[t, 1],
-            device_id=(d, place(t)),
-            device_id_type=MESH,
-        )
 
     khalf = kwidth // 2
 
@@ -383,13 +379,14 @@
                         c.start()
             if s == m and slot - lag == last - 1:
                 key_finish()
-        step = slot - lags[-1] - 1
+        step = slot - lags[-1] - 1 - layout.index(None)
         if 0 <= step < m:
             gather_next(step)
 
-    for t in range(n_units - parts):
-        a2a(t).wait_send()
-        a2a(t).wait_recv()
+    for w in units:
+        if not w.key and not w.mine:
+            w.exchange.wait_send()
+            w.exchange.wait_recv()
     for s in range(m):
         for c in gather_copies(s):
             c.wait_send()
@@ -398,13 +395,17 @@
 
 def finish(n_ex, slot, *refs):
     sources, targets, sems = refs[:8], refs[8:16], refs[16]
-    copies = []
-    for i in (0, 1, 2, 7, 3, 4, 5):
-        copies.append(pltpu.make_async_copy(sources[i], targets[i], sems.at[i]))
+    pairs = []
+    for i in range(3):
+        part = sources[i].shape[1] // 4
+        for k in range(4):
+            at = pl.ds(k * part, part)
+            pairs.append((sources[i].at[:, at], targets[i].at[:, at]))
+    for i in (7, 3, 4, 5):
+        pairs.append((sources[i], targets[i]))
     for e in range(n_ex):
-        copies.append(
-            pltpu.make_async_copy(sources[6].at[e], targets[6].at[slot[e]], sems.at[8 + e])
-        )
+        pairs.append((sources[6].at[e], targets[6].at[slot[e]]))
+    copies = [pltpu.make_async_copy(a, b, sems.at[i]) for i, (a, b) in enumerate(pairs)]
     for c in copies:
         c.start()
     for c in copies:
@@ -434,8 +435,7 @@
         krows, kwidth = key_param.shape
         key_rows = key_partials.shape[1]
         cw = width // n_ex
-        parts = parts_of(cw)
-        n_units, uw = n_ex * parts, cw // parts
+        layout = plan(n_ex, cw)
         eg = expert_partials.reshape(chips, 2, rows, width)
         kg = key_partials.reshape(chips, 2, krows, kwidth)
         shape = jax.ShapeDtypeStruct
@@ -444,7 +444,16 @@
         scalars = pl.BlockSpec(memory_space=pltpu.SMEM)
         vector = pl.BlockSpec(memory_space=pltpu.VMEM)
         dma = pltpu.SemaphoreType.DMA
-        counts = [2 ** (m - 1 - s) for s in range(m)]
+        buffers = []
+        for entry in layout:
+            high, wide = (krows, kwidth) if entry is None else (rows, entry[2])
+            buffers += [pltpu.VMEM((chips, high, wide), t) for t in (F32, F32, BF16, BF16)]
+            steps = [
+                pltpu.VMEM((2, 2 ** (m - 1 - s), high // 2, wide), BF16) for s in range(m)
+            ]
+            buffers += steps + steps
+            if entry is not None and entry[0] < n_ex - 1:
+                buffers.append(pltpu.VMEM((high, wide), BF16))
         here = functools.partial(pltpu.with_memory_space_constraint, memory_space=pltpu.HBM)
         out = pl.pallas_call(
             functools.partial(kernel, n_dp, n_ex),
@@ -454,31 +463,19 @@
             in_specs=[hbm] * 11,
             out_specs=[vector] * 8,
             scratch_shapes=[
-                pltpu.VMEM((n_units, chips, rows, uw), F32),
-                pltpu.VMEM((n_units, chips, rows, uw), F32),
-                pltpu.VMEM((n_units, chips, rows, uw), BF16),
-                pltpu.VMEM((n_units, chips, rows, uw), BF16),
-                pltpu.VMEM((n_units - parts, rows, uw), BF16),
-                pltpu.VMEM((chips, krows, kwidth), F32),
-                pltpu.VMEM((chips, krows, kwidth), F32),
-                pltpu.VMEM((chips, krows, kwidth), BF16),
-                pltpu.VMEM((chips, krows, kwidth), BF16),
                 pltpu.VMEM((chips, 2, krows, kwidth), BF16),
                 pltpu.SMEM(expert_scales.shape[1:2] + (n_ex,) + expert_scales.shape[2:], F32),
                 pltpu.SMEM(key_scales.shape, F32),
                 pltpu.VMEM((1, HD), jnp.int32),
-            ]
-            + [pltpu.VMEM((n_units, 2, c, rows, uw // 2), BF16) for c in counts] * 2
-            + [pltpu.VMEM((2, c, krows, kwidth // 2), BF16) for c in counts] * 2
-            + [
-                dma((n_units + 1, 5)),
-                dma((n_units + 1, 2)),
-                dma((n_units + 1, m, 2, 2)),
-                dma((n_units - parts, 2)),
+                dma((len(layout), 5)),
+                dma((len(layout), 2)),
+                dma((len(layout), m, 2, 2)),
+                dma((len(layout), 2)),
                 dma((m, 2, 2 ** (m - 1), 2)),
                 dma((2,)),
                 dma((3,)),
-            ],
+            ]
+            + buffers,
             compiler_params=pltpu.CompilerParams(
                 collective_id=0, has_side_effects=True, vmem_limit_bytes=int(46 * 2**20)
             ),
@@ -506,7 +503,7 @@
             out_shape=[shape(x.shape, x.dtype) for x in out],
             in_specs=[scalars] + [vector] * 8,
             out_specs=[anywhere] * 8,
-            scratch_shapes=[dma((8 + n_ex,))],
+            scratch_shapes=[dma((16 + n_ex,))],
             compiler_params=pltpu.CompilerParams(vmem_limit_bytes=16 * 2**20),
             name="finish",
         )(expert_slot, *out)

time: 51.9 us -> 51.9 us (level)
  no operation moved by 1% of the time
where the time goes in v4:
time: 51.9 us; the launch traced here: 51.8 us
  Pallas kernels  51.1 us (98%)
  between operations  0.66 us (1%)
    pallas_call x1, Pallas kernels, on_device(): pl.pallas_call(functools.partial(kernel, n_dp, n_ex), out_shape=[shape(ex...  47.5 us
    pallas_call x1, Pallas kernels, on_device(): pl.pallas_call(functools.partial(finish, n_ex), out_shape=[shape(x.shape,...  3.67 us

profile of v4, /device:TPU:0, one launch (start us, length us, event | category | flops | bytes accessed | tf_op | source)
XLA Modules:
  0.0 51.8 jit_solution(1363076190252573983)
XLA Ops:
  0.6 0.0 copy-start
  0.6 47.5 %reduce_update_exchange.1 = (f32[1,192,2048]{2,1,0:T(8,128)S(1)}, f32[1,192,2048]{2,1,0:T(8,128)S(1)}, f32[1,192,2048]{2,1,0:T(8,128)S(1)}, f32[64,1024]{1,0:T(8...) custom-call(f32[4,2,192,2048]{3,2,1,0:T(8,128)} %bitcast.5, ...), custom_call_target="tpu_custom_call" | custom-call | tf_op jit(solution)/shard_map/reduce_update_exchange/pallas_call | solution.py:458
  48.1 0.0 copy-done
  48.1 3.7 %finish.1 = (f32[1,192,2048]{2,1,0:T(8,128)}, f32[1,192,2048]{2,1,0:T(8,128)}, f32[1,192,2048]{2,1,0:T(8,128)}, f32[64,1024]{1,0:T(8,128)}, f32[64,1024]{1,0:T(8...) custom-call(s32[4]{0:T(128)S(1)} %copy-done, ...), custom_call_target="tpu_custom_call" | custom-call | tf_op jit(solution)/shard_map/finish/pallas_call | solution.py:501
Async XLA Ops:
  0.6 47.5 %copy-start = (s32[4]{0:T(128)S(1)}, s32[4]{0:T(128)}, u32[]{:S(2)}) copy-start(s32[4]{0:T(128)} %slot.1) | copy-start | bytes 52

commit v5 on v4

--- a/solution.py
+++ b/solution.py
@@ -86,8 +86,8 @@
 ):
     chips = n_dp // 2
     m = chips.bit_length() - 1
-    load_sem, s0_sem, rs_sem, a2a_sem, ag_sem, pair_sem, small_sem = rest[:7]
-    rest = list(rest[7:])
+    load_sem, s0_sem, rs_sem, a2a_sem, ag_sem, pair_sem, small_sem, ready = rest[:8]
+    rest = list(rest[8:])
 
     d = lax.axis_index("dp")
     z = lax.axis_index("expert")
@@ -200,10 +200,43 @@
                 c.start()
 
     barrier = pltpu.get_barrier_semaphore()
-    peers = [(other_core, z)] + [(partner(i), z) for i in range(m)]
-    peers += [(d, (z + k) % n_ex) for k in range(1, n_ex)]
-    for peer in peers:
-        pl.semaphore_signal(barrier, inc=1, device_id=peer, device_id_type=MESH)
+    for k in range(1, chips):
+        pl.semaphore_signal(
+            barrier, inc=1, device_id=((chip + k) % chips * 2, z), device_id_type=MESH
+        )
+
+    @pl.when(core == 1)
+    def _():
+        pl.semaphore_signal(barrier, inc=1, device_id=(other_core, z), device_id_type=MESH)
+
+    def plane_ready():
+        @pl.when(core == 0)
+        def _():
+            pl.semaphore_wait(barrier, 2 * chips - 1)
+            pl.semaphore_signal(
+                ready.at[0], inc=1, device_id=(other_core, z), device_id_type=MESH
+            )
+
+        @pl.when(core == 1)
+        def _():
+            pl.semaphore_wait(ready.at[0], 1)
+            for k in range(1, n_ex):
+                pl.semaphore_signal(
+                    barrier, inc=1, device_id=(d, (z + k) % n_ex), device_id_type=MESH
+                )
+
+    def planes_ready():
+        @pl.when(core == 1)
+        def _():
+            pl.semaphore_wait(barrier, n_ex - 1)
+            pl.semaphore_signal(
+                ready.at[1], inc=1, device_id=(other_core, z), device_id_type=MESH
+            )
+
+        @pl.when(core == 0)
+        def _():
+            pl.semaphore_wait(ready.at[1], 1)
+
     load(0)
     load(1)
 
@@ -239,7 +272,7 @@
 
         loop(chips * per, body)
         if w.u == 0:
-            pl.semaphore_wait(barrier, len(peers))
+            plane_ready()
         w.s0.start()
 
     def reduce(w, s):
@@ -299,6 +332,8 @@
         if w.key:
             gather_send(0)
         elif not w.mine:
+            if w.u == 0:
+                planes_ready()
             w.exchange.start()
         w.s0.wait_send()
         for s in range(m):
@@ -365,7 +400,7 @@
                 o_key[cols, head * HD : (head + 1) * HD] = turned.astype(BF16)
 
     stages = [first] + [functools.partial(reduce, s=s) for s in range(m)] + [update]
-    lags = [0, 1] + [1 + 2 * s for s in range(1, m)] + [2 * m]
+    lags = [0, 1] + [2 + 2 * s for s in range(1, m)] + [2 * m + 1]
     last = len(units) - 1
     for slot in range(len(units) + lags[-1]):
         for s, (stage, lag) in enumerate(zip(stages, lags)):
@@ -474,6 +509,7 @@
                 dma((m, 2, 2 ** (m - 1), 2)),
                 dma((2,)),
                 dma((3,)),
+                pltpu.SemaphoreType.REGULAR((2,)),
             ]
             + buffers,
             compiler_params=pltpu.CompilerParams(

time: 51.9 us -> 52.6 us (1.013)
  Pallas kernels: 51.1 us -> 51.8 us
    pallas_call x1, Pallas kernels: 47.5 us -> 48.2 us  [on_device(): pl.pallas_call(functools.partial(kernel, n_dp, n_ex), out_shape=[shape(ex...]
where the time goes in v5:
time: 52.6 us; the launch traced here: 52.5 us
  Pallas kernels  51.8 us (98%)
  between operations  0.66 us (1%)
    pallas_call x1, Pallas kernels, on_device(): pl.pallas_call(functools.partial(kernel, n_dp, n_ex), out_shape=[shape(ex...  48.2 us
    pallas_call x1, Pallas kernels, on_device(): pl.pallas_call(functools.partial(finish, n_ex), out_shape=[shape(x.shape,...  3.67 us

profile of v5, /device:TPU:0, one launch (start us, length us, event | category | flops | bytes accessed | tf_op | source)
XLA Modules:
  0.0 52.5 jit_solution(9684663954031719842)
XLA Ops:
  0.6 0.0 copy-start
  0.6 48.2 %reduce_update_exchange.1 = (f32[1,192,2048]{2,1,0:T(8,128)S(1)}, f32[1,192,2048]{2,1,0:T(8,128)S(1)}, f32[1,192,2048]{2,1,0:T(8,128)S(1)}, f32[64,1024]{1,0:T(8...) custom-call(f32[4,2,192,2048]{3,2,1,0:T(8,128)} %bitcast.5, ...), custom_call_target="tpu_custom_call" | custom-call | tf_op jit(solution)/shard_map/reduce_update_exchange/pallas_call | solution.py:493
  48.8 0.0 copy-done
  48.8 3.7 %finish.1 = (f32[1,192,2048]{2,1,0:T(8,128)}, f32[1,192,2048]{2,1,0:T(8,128)}, f32[1,192,2048]{2,1,0:T(8,128)}, f32[64,1024]{1,0:T(8,128)}, f32[64,1024]{1,0:T(8...) custom-call(s32[4]{0:T(128)S(1)} %copy-done, ...), custom_call_target="tpu_custom_call" | custom-call | tf_op jit(solution)/shard_map/finish/pallas_call | solution.py:537
Async XLA Ops:
  0.6 48.2 %copy-start = (s32[4]{0:T(128)S(1)}, s32[4]{0:T(128)}, u32[]{:S(2)}) copy-start(s32[4]{0:T(128)} %slot.1) | copy-start | bytes 52

commit v6 on v5

--- a/solution.py
+++ b/solution.py
@@ -37,6 +37,15 @@
         return carry
 
     lax.fori_loop(0, count, step, 0)
+
+
+def dest_of(z, n_ex, t):
+    if n_ex != 4:
+        return (z + n_ex - 1 - t) % n_ex
+    side = z // 2
+    near = z + side * (3 - 2 * z)
+    dest = (3, 2 - 2 * near, 1 + near, near)[t]
+    return dest + side * (3 - 2 * dest)
 
 
 def plan(n_ex, cw):
@@ -86,8 +95,8 @@
 ):
     chips = n_dp // 2
     m = chips.bit_length() - 1
-    load_sem, s0_sem, rs_sem, a2a_sem, ag_sem, pair_sem, small_sem, ready = rest[:8]
-    rest = list(rest[8:])
+    load_sem, s0_sem, rs_sem, a2a_sem, ag_sem, pair_sem, small_sem, arrive_sem, ready = rest[:9]
+    rest = list(rest[9:])
 
     d = lax.axis_index("dp")
     z = lax.axis_index("expert")
@@ -132,7 +141,7 @@
         else:
             t, w.at, w.cols = entry
             w.rows = rows
-            w.dest = (z + n_ex - 1 - t) % n_ex
+            w.dest = dest_of(z, n_ex, t)
             w.mine = t == n_ex - 1
             w.columns = pl.ds(pl.multiple_of(w.dest * cw + w.at, BLOCK), w.cols)
             w.grad = eg_hbm
@@ -143,8 +152,8 @@
                 w.exchange = pltpu.make_async_remote_copy(
                     src_ref=w.grid,
                     dst_ref=o_arr.at[z, :, pl.ds(w.at, w.cols)],
-                    send_sem=a2a_sem.at[u, 0],
-                    recv_sem=a2a_sem.at[u, 1],
+                    send_sem=a2a_sem.at[u],
+                    recv_sem=arrive_sem.at[z],
                     device_id=(d, w.dest),
                     device_id_type=MESH,
                 )
@@ -400,7 +409,7 @@
                 o_key[cols, head * HD : (head + 1) * HD] = turned.astype(BF16)
 
     stages = [first] + [functools.partial(reduce, s=s) for s in range(m)] + [update]
-    lags = [0, 1] + [2 + 2 * s for s in range(1, m)] + [2 * m + 1]
+    lags = [0, 1] + [1 + 2 * s for s in range(1, m)] + [2 * m]
     last = len(units) - 1
     for slot in range(len(units) + lags[-1]):
         for s, (stage, lag) in enumerate(zip(stages, lags)):
@@ -418,10 +427,19 @@
         if 0 <= step < m:
             gather_next(step)
 
+    for k in range(1, n_ex):
+        source = (z + k) % n_ex
+        pltpu.make_async_remote_copy(
+            src_ref=o_arr.at[source],
+            dst_ref=o_arr.at[source],
+            send_sem=a2a_sem.at[0],
+            recv_sem=arrive_sem.at[source],
+            device_id=(d, source),
+            device_id_type=MESH,
+        ).wait_recv()
     for w in units:
         if not w.key and not w.mine:
             w.exchange.wait_send()
-            w.exchange.wait_recv()
     for s in range(m):
         for c in gather_copies(s):
             c.wait_send()
@@ -505,10 +523,11 @@
                 dma((len(layout), 5)),
                 dma((len(layout), 2)),
                 dma((len(layout), m, 2, 2)),
-                dma((len(layout), 2)),
+                dma((len(layout),)),
                 dma((m, 2, 2 ** (m - 1), 2)),
                 dma((2,)),
                 dma((3,)),
+                dma((n_ex,)),
                 pltpu.SemaphoreType.REGULAR((2,)),
             ]
             + buffers,

time: 52.6 us -> 50.1 us (0.952)
  Pallas kernels: 51.8 us -> 49.3 us
    pallas_call x1, Pallas kernels: 48.2 us -> 45.6 us  [on_device(): pl.pallas_call(functools.partial(kernel, n_dp, n_ex), out_shape=[shape(ex...]
where the time goes in v6:
time: 50.1 us; the launch traced here: 50 us
  Pallas kernels  49.3 us (98%)
  between operations  0.66 us (1%)
    pallas_call x1, Pallas kernels, on_device(): pl.pallas_call(functools.partial(kernel, n_dp, n_ex), out_shape=[shape(ex...  45.6 us
    pallas_call x1, Pallas kernels, on_device(): pl.pallas_call(functools.partial(finish, n_ex), out_shape=[shape(x.shape,...  3.67 us

profile of v6, /device:TPU:0, one launch (start us, length us, event | category | flops | bytes accessed | tf_op | source)
XLA Modules:
  0.0 50.0 jit_solution(18219401507133892253)
XLA Ops:
  0.6 0.0 copy-start
  0.6 45.6 %reduce_update_exchange.1 = (f32[1,192,2048]{2,1,0:T(8,128)S(1)}, f32[1,192,2048]{2,1,0:T(8,128)S(1)}, f32[1,192,2048]{2,1,0:T(8,128)S(1)}, f32[64,1024]{1,0:T(8...) custom-call(f32[4,2,192,2048]{3,2,1,0:T(8,128)} %bitcast.5, ...), custom_call_target="tpu_custom_call" | custom-call | tf_op jit(solution)/shard_map/reduce_update_exchange/pallas_call | solution.py:511
  46.3 0.0 copy-done
  46.3 3.7 %finish.1 = (f32[1,192,2048]{2,1,0:T(8,128)}, f32[1,192,2048]{2,1,0:T(8,128)}, f32[1,192,2048]{2,1,0:T(8,128)}, f32[64,1024]{1,0:T(8,128)}, f32[64,1024]{1,0:T(8...) custom-call(s32[4]{0:T(128)S(1)} %copy-done, ...), custom_call_target="tpu_custom_call" | custom-call | tf_op jit(solution)/shard_map/finish/pallas_call | solution.py:556
Async XLA Ops:
  0.6 45.6 %copy-start = (s32[4]{0:T(128)S(1)}, s32[4]{0:T(128)}, u32[]{:S(2)}) copy-start(s32[4]{0:T(128)} %slot.1) | copy-start | bytes 52
